TPU v7x, 32 devices: a whole 2x2x4 slice. The times are simulated.
32 devices in a mesh: gx: 4 (over z), gy: 4 (over y, x), gz: 2 (over core).
Axes of the slice: x: 2, y: 2, z: 4, core: 2. Of those that a mesh axis runs over, the one named last changes fastest.
Arguments:
- features: bfloat16 [8192, 1024], P(('gx', 'gy', 'gz')), may hold values from -6 to 6
- cotangent: bfloat16 [8192, 1024], P(('gx', 'gy', 'gz')), may hold values from -6 to 6
- leaf_device: int32 [8192, 1], P(('gx', 'gy', 'gz')), may hold values from 0 to 31; in each aligned block of 256 rows (0 to 255, 256 to 511, ...) at most 16 rows name the same one
- neighbours: int32 [16, 16384], P(None, ('gx', 'gy', 'gz')), may hold values from 0 to 511
- radial: float32 [64, 16384], P(None, ('gx', 'gy', 'gz')), may hold values from 0.25 to 2
- first_zero: bfloat16 [256, 256], replicated, may hold values from -0.375 to 0.375
- first_one: bfloat16 [192, 192], replicated, may hold values from -0.4375 to 0.4375
- first_two: bfloat16 [128, 128], replicated, may hold values from -0.5 to 0.5
- first_three: bfloat16 [64, 64], replicated, may hold values from -0.75 to 0.75
- second_zero: bfloat16 [256, 256], replicated, may hold values from -0.375 to 0.375
- second_one: bfloat16 [192, 192], replicated, may hold values from -0.4375 to 0.4375
- second_two: bfloat16 [128, 128], replicated, may hold values from -0.5 to 0.5
- second_three: bfloat16 [64, 64], replicated, may hold values from -0.75 to 0.75
- lift_leaf: float32 [2, 16, 16], replicated, may hold values from -1 to 1
- lift_branch: float32 [4, 16, 16], replicated, may hold values from -0.75 to 0.75
- couple_root: float32 [4, 4, 16, 16], replicated, may hold values from -0.75 to 0.75
- couple_branch: float32 [4, 4, 16, 16], replicated, may hold values from -0.75 to 0.75
- couple_leaf: float32 [2, 2, 16, 16], replicated, may hold values from -1 to 1
Outputs:
- updated: bfloat16 [8192, 1024], P(('gx', 'gy', 'gz'))
- radial_grad: float32 [64, 16384], P(None, ('gx', 'gy', 'gz'))
Inputs may be any that keep to these rules, and one draw needn't show every extreme that they name: `leaf_device`: among the 256 atoms of one brick at most 16 have the same leaf; every leaf holds at least one atom.
All inputs are finite; a program needn't handle non-finite values.
Results may differ from a plain program's by a relative error of at most 0.0037.
Values may be sent and summed in bfloat16 or wider, within the bound.
A program may use at most 64 MiB of HBM per device.

v0:
```python
import math

import jax
import jax.numpy as jnp
import numpy as np
from jax import lax
from jax.sharding import PartitionSpec as P

DEGREES = (0, 1, 2, 3, 1, 2, 3, 1, 2, 3, 2, 3, 2, 3, 3, 3)
BLOCKS = ((0, 4, 0), (4, 7, 1), (7, 10, 1), (10, 12, 2), (12, 14, 2), (14, 15, 3), (15, 16, 3))


def degree_table(chans):
    table = np.zeros((4, 16 * chans), dtype=np.float32)
    for coef, degree in enumerate(DEGREES):
        table[degree, coef * chans : (coef + 1) * chans] = 1.0
    return jnp.asarray(table)


def mixing(values, mats, flip):
    chans = mats[3].shape[0]
    outs = []
    for first, last, which in BLOCKS:
        piece = values[:, first * chans : last * chans]
        weight = mats[which]
        if flip:
            result = lax.dot_general(
                piece, weight, (((1,), (1,)), ((), ())), preferred_element_type=jnp.float32
            )
        else:
            result = jnp.dot(piece, weight, preferred_element_type=jnp.float32)
        outs.append(result)
    return jnp.concatenate(outs, axis=1)


def shards(
    features,
    cotangent,
    leaf_device,
    neighbours,
    radial,
    first_zero,
    first_one,
    first_two,
    first_three,
    second_zero,
    second_one,
    second_two,
    second_three,
    lift_leaf,
    lift_branch,
    couple_root,
    couple_branch,
    couple_leaf,
):
    hp = lax.Precision.HIGHEST
    rows, width = features.shape
    chans = width // 16
    size_x = lax.axis_size("gx")
    size_y = lax.axis_size("gy")
    size_z = lax.axis_size("gz")
    devices = size_x * size_y * size_z
    pool = neighbours.shape[1]
    cap = pool // devices
    target = leaf_device[:, 0]
    onehot = (target[:, None] == jnp.arange(devices, dtype=jnp.int32)[None, :]).astype(jnp.int32)
    rank = jnp.sum(jnp.cumsum(onehot, axis=0) * onehot, axis=1) - 1
    slot = target * cap + rank
    send_feat = jnp.zeros((pool, width), jnp.bfloat16).at[slot].set(features)
    send_grad = jnp.zeros((pool, width), jnp.bfloat16).at[slot].set(cotangent)
    send_mask = jnp.zeros((pool,), jnp.bfloat16).at[slot].set(jnp.ones((rows,), jnp.bfloat16))
    flat_shape = (devices, cap * width)
    got_feat, got_grad, got_mask = (
        lax.all_to_all(
            send_feat.reshape(flat_shape),
            ("gx", "gy", "gz"),
            split_axis=0,
            concat_axis=0,
            tiled=True,
        ),
        lax.all_to_all(
            send_grad.reshape(flat_shape),
            ("gx", "gy", "gz"),
            split_axis=0,
            concat_axis=0,
            tiled=True,
        ),
        lax.all_to_all(
            send_mask.reshape(devices, cap),
            ("gx", "gy", "gz"),
            split_axis=0,
            concat_axis=0,
            tiled=True,
        ),
    )
    pool_feat = got_feat.reshape(pool, width)
    pool_grad = got_grad.reshape(pool, width)
    occ_int = got_mask.reshape(pool).astype(jnp.int32)
    occ = occ_int.astype(jnp.float32)
    order = jnp.argsort(1 - occ_int, stable=True)
    filled = jnp.sum(occ_int)
    leaf = jnp.sum(pool_feat, axis=0, dtype=jnp.float32).reshape(16, chans) / math.sqrt(rows)
    index_x = lax.axis_index("gx")
    index_y = lax.axis_index("gy")
    index_z = lax.axis_index("gz")
    sib_leaf = lax.all_gather(leaf[None], "gz", axis=0, tiled=True)
    middle = jnp.einsum("kpq,kqc->pc", lift_leaf, sib_leaf, precision=hp)
    sib_branch = lax.all_gather(middle[None], "gy", axis=0, tiled=True)
    topmost = jnp.einsum("kpq,kqc->pc", lift_branch, sib_branch, precision=hp)
    sib_root = lax.all_gather(topmost[None], "gx", axis=0, tiled=True)
    root_mask = couple_root * (1.0 - jnp.eye(size_x, dtype=jnp.float32))[:, :, None, None]
    branch_mask = couple_branch * (1.0 - jnp.eye(size_y, dtype=jnp.float32))[:, :, None, None]
    leaf_mask = couple_leaf * (1.0 - jnp.eye(size_z, dtype=jnp.float32))[:, :, None, None]
    local1 = jnp.einsum("jpq,jqc->pc", root_mask[index_x], sib_root, precision=hp)
    local2 = jnp.einsum("qp,qc->pc", lift_branch[index_y], local1, precision=hp) + jnp.einsum(
        "jpq,jqc->pc", branch_mask[index_y], sib_branch, precision=hp
    )
    local3 = jnp.einsum("qp,qc->pc", lift_leaf[index_z], local2, precision=hp) + jnp.einsum(
        "jpq,jqc->pc", leaf_mask[index_z], sib_leaf, precision=hp
    )
    firsts = (first_zero, first_one, first_two, first_three)
    seconds = (second_zero, second_one, second_two, second_three)
    table = degree_table(chans)
    trans = mixing(pool_grad, seconds, True)
    feat = pool_feat.astype(jnp.float32)

    def step(carry, item):
        choose, rad4 = item
        index = order[choose % filled]
        other = pool_feat[index]
        summed = feat + other.astype(jnp.float32)
        expand = lax.dot_general(rad4, table, (((0,), (0,)), ((), ())), precision=hp)
        zeta = (summed * expand).astype(jnp.bfloat16)
        upper = mixing(zeta, firsts, False)
        value = jax.nn.silu(upper).astype(jnp.bfloat16)
        message = mixing(value, seconds, False)
        sig = jax.nn.sigmoid(upper)
        grad_u = (sig * (1.0 + upper * (1.0 - sig)) * trans).astype(jnp.bfloat16)
        back = mixing(grad_u, firsts, True)
        dradial = (
            0.25
            * occ[None, :]
            * lax.dot_general(table, back * summed, (((1,), (1,)), ((), ())), precision=hp)
        )
        return (carry + message, dradial)

    near, grads = lax.scan(
        step, jnp.zeros((pool, width), jnp.float32), (neighbours, radial.reshape(-1, 4, pool))
    )
    near = 0.25 * occ[:, None] * near
    pool_out = (feat + near + feat * local3.reshape(1, width)).astype(jnp.bfloat16)
    returned = lax.all_to_all(
        pool_out.reshape(flat_shape), ("gx", "gy", "gz"), split_axis=0, concat_axis=0, tiled=True
    )
    updated = returned.reshape(pool, width)[slot]
    return (updated, grads.reshape(-1, pool))


def solution(mesh):
    placed = (
        P(("gx", "gy", "gz"), None),
        P(("gx", "gy", "gz"), None),
        P(("gx", "gy", "gz"), None),
        P(None, ("gx", "gy", "gz")),
        P(None, ("gx", "gy", "gz")),
        P(),
        P(),
        P(),
        P(),
        P(),
        P(),
        P(),
        P(),
        P(),
        P(),
        P(),
        P(),
        P(),
    )
    return jax.shard_map(
        shards,
        mesh=mesh,
        in_specs=placed,
        out_specs=(P(("gx", "gy", "gz"), None), P(None, ("gx", "gy", "gz"))),
        check_vma=False,
    )
```

profile of v0, /device:TPU:27, one launch (start us, length us, event | category | flops | bytes accessed | tf_op | source)
XLA Modules:
  0.0 831.7 jit_solution(16594438711836759266)
XLA Ops:
  6.5 6.2 all-to-all-start.1
  16.5 7.0 reduce.15
  25.1 6.2 all-to-all-start
  38.6 8.0 reduce.16
  49.2 5.2 all-to-all-done
  54.5 7.2 all-to-all-start.2
  73.7 7.7 reduce.3
  84.8 5.9 reshape.267
  90.8 8.7 %reduce.6 = bf16[32,16384]{1,0:T(8,128)(2,1)} reduce(bf16[32,1,16384]{2,1,0:T(2,128)(2,1)} %reshape.267, bf16[]{:T(256)} %constant.93), dimensions={1}, to_apply=%all_to_all.29.reduce_sub_computation | reduce | bytes 2097154 | tf_op jit(solution)/shard_map/all_to_all | solution.py:81
  108.0 640.9 %while.16 = (s32[]{:T(128)}, f32[512,1024]{0,1:T(8,128)}, f32[16,4,512]{2,1,0:T(4,128)}, s32[16,512]{1,0:T(8,128)}, s32[]{:T(128)}, /*index=5*/pred[]{:T(512)}, ...) while((s32[]{:T(128)}, f32[512,1024]{0,1:T(8,128)}, ...), condition=%wide.region_9.10_spmd.clone.clone, body=%wide.region_8.9_spmd.sunk.clone.clone.sunk | while | flops 614476800 | bytes 53696004 | solution.py:147
  132.8 4.7 fusion.223
  172.3 4.7 fusion.223
  212.4 4.7 fusion.223
  252.5 4.7 fusion.223
  292.6 4.7 fusion.223
  332.6 4.7 fusion.223
  372.7 4.7 fusion.223
  412.8 4.7 fusion.223
  753.8 6.1 all-gather
  760.1 10.2 %all-gather.1 = f32[64,64]{1,0:T(8,128)S(1)} all-gather(f32[16,64]{1,0:T(8,128)S(1)} %convolution_bitcast_fusion.3), channel_id=3, replica_groups=mesh['gx'=4,'gy'=4,'gz'=2] {'gx'}, dimensions={0}, use_global_device_ids=true | all-gather | bytes 20480 | tf_op jit(solution)/shard_map/all_gather | solution.py:110
  779.2 7.0 reduce.17
  787.8 10.2 %all-to-all-start.3 = ((bf16[32,2,8192]{2,1,0:T(2,128)(2,1)}), bf16[32,2,8192]{2,1,0:T(2,128)(2,1)S(1)}, u32[]{:S(2)}, u32[]{:S(2)}) async-start(bf16[32,2,8192]{2,1,0:T(2,128)(2,1)} %reshape.268), calls=%async_computation.3 | async-start | bytes 2097152 | tf_op jit(solution)/shard_map/all_to_all | solution.py:152
  798.7 22.5 %all-to-all-done.3 = bf16[32,2,8192]{2,1,0:T(2,128)(2,1)S(1)} async-done(((bf16[32,2,8192]{2,1,0:T(2,128)(2,1)}), bf16[32,2,8192]{2,1,0:T(2,128)(2,1)S(1)}, u32[]{:S(2)}, u32[]{:S(2)}) %all-to-all-start.3) | async-done | bytes 1048608 | tf_op jit(solution)/shard_map/all_to_all | solution.py:152
  822.3 6.4 reduce.7
  (944 shorter events, 663.8 us)
Async XLA Ops:
  0.6 759.3 %copy-start = (f32[4,16,16]{2,1,0:T(8,128)S(1)}, f32[4,16,16]{2,1,0:T(8,128)}, u32[]{:S(2)}) copy-start(f32[4,16,16]{2,1,0:T(8,128)} %param.35) | copy-start | bytes 12292
  3.6 27.6 %copy-start.24 = (s32[256,1]{0,1:T(1,128)}, s32[256,1]{0,1:T(1,128)S(1)}, u32[]{:S(2)}) copy-start(s32[256,1]{0,1:T(1,128)S(1)} %compare_select_fusion.2) | copy-start | bytes 3076
  6.5 18.6 %all-to-all-start.1 = ((bf16[32,1,16]{2,1,0:T(2,128)(2,1)}), bf16[32,1,16]{2,1,0:T(2,128)(2,1)S(1)}, u32[]{:S(2)}, u32[]{:S(2)}) async-start(bf16[32,1,16]{2,1,0:T(2,128)(2,1)} %all_to_all.33), calls=%async_computation.1 | async-start | bytes 32768 | tf_op jit(solution)/shard_map/all_to_all | solution.py:88
  25.1 29.4 %all-to-all-start = ((bf16[32,2,8192]{2,1,0:T(2,128)(2,1)}), bf16[32,2,8192]{2,1,0:T(2,128)(2,1)S(1)}, u32[]{:S(2)}, u32[]{:S(2)}) async-start(bf16[32,2,8192]{2,1,0:T(2,128)(2,1)} %reshape.264), calls=%async_computation | async-start | bytes 2097152 | tf_op jit(solution)/shard_map/all_to_all | solution.py:74
  46.6 15.1 %copy-start.20 = (f32[64,512]{1,0:T(8,128)S(1)}, f32[64,512]{1,0:T(8,128)}, u32[]{:S(2)}) copy-start(f32[64,512]{1,0:T(8,128)} %param.25) | copy-start | bytes 393220
  54.5 14.9 %copy-start.16 = (bf16[32,2,8192]{2,1,0:T(2,128)(2,1)}, bf16[32,2,8192]{2,1,0:T(2,128)(2,1)S(1)}, u32[]{:S(2)}) copy-start(bf16[32,2,8192]{2,1,0:T(2,128)(2,1)S(1)} %all-to-all-done) | copy-start | bytes 3145732
  54.5 30.4 %all-to-all-start.2 = ((bf16[32,2,8192]{2,1,0:T(2,128)(2,1)}), bf16[32,2,8192]{2,1,0:T(2,128)(2,1)}, u32[]{:S(2)}, u32[]{:S(2)}) async-start(bf16[32,2,8192]{2,1,0:T(2,128)(2,1)} %reshape.266), calls=%async_computation.2 | async-start | bytes 2097152 | tf_op jit(solution)/shard_map/all_to_all | solution.py:81
  101.9 6.1 copy-start.4
  101.9 6.1 copy-start.7
  101.9 6.1 copy-start.9
  132.8 5.8 copy-start.6
  172.3 5.8 copy-start.6
  212.4 5.8 copy-start.6
  252.5 5.8 copy-start.6
  292.5 5.8 copy-start.6
  332.6 5.8 copy-start.6
  372.7 5.8 copy-start.6
  749.0 21.4 %copy-start.27 = (f32[1,4]{1,0:T(1,128)S(1)}, f32[1,4]{1,0:T(1,128)}, u32[]{:S(2)}) copy-start(f32[1,4]{1,0:T(1,128)} %get-tuple-element.430) | copy-start | bytes 52
  749.0 22.4 %copy-start.26 = (f32[1,4]{1,0:T(1,128)S(1)}, f32[1,4]{1,0:T(1,128)}, u32[]{:S(2)}) copy-start(f32[1,4]{1,0:T(1,128)} %get-tuple-element.429) | copy-start | bytes 52
  749.0 23.7 %copy-start.23 = (f32[2,2,16,16]{3,2,1,0:T(8,128)S(1)}, f32[2,2,16,16]{3,2,1,0:T(8,128)}, u32[]{:S(2)}) copy-start(f32[2,2,16,16]{3,2,1,0:T(8,128)} %param.38) | copy-start | bytes 12292
  749.0 23.7 %copy-start.28 = (f32[1,2]{1,0:T(1,128)S(1)}, f32[1,2]{1,0:T(1,128)}, u32[]{:S(2)}) copy-start(f32[1,2]{1,0:T(1,128)} %constant_dynamic-slice_fusion) | copy-start | bytes 28
  786.1 11.9 %copy-start.25 = (s32[256,1]{0,1:T(1,128)S(1)}, s32[256,1]{0,1:T(1,128)}, u32[]{:S(2)}) copy-start(s32[256,1]{0,1:T(1,128)} %copy-done.24) | copy-start | bytes 3076
  786.2 11.9 %copy-start.21 = (f32[16,4,512]{2,1,0:T(4,128)S(1)}, f32[16,4,512]{2,1,0:T(4,128)}, u32[]{:S(2)}) copy-start(f32[16,4,512]{2,1,0:T(4,128)} %get-tuple-element.677) | copy-start | bytes 393220
  787.8 33.4 %all-to-all-start.3 = ((bf16[32,2,8192]{2,1,0:T(2,128)(2,1)}), bf16[32,2,8192]{2,1,0:T(2,128)(2,1)S(1)}, u32[]{:S(2)}, u32[]{:S(2)}) async-start(bf16[32,2,8192]{2,1,0:T(2,128)(2,1)} %reshape.268), calls=%async_computation.3 | async-start | bytes 2097152 | tf_op jit(solution)/shard_map/all_to_all | solution.py:152
  (159 other events, 580.2 us)
where the time goes:
time: 848 us; the launch traced here: 832 us
  matrix products  371 us (44%)
  local copies, waits for them, and re-layouts  214 us (25%)
  other arithmetic  164 us (19%)
  starting transfers between devices  29.7 us (4%)
  waiting for transfers between devices  29.1 us (3%)
  blocking collectives  18.9 us (2%)
    dot_general x224, matrix products, mixing(): result = jnp.dot(piece, weight, preferred_element_type=jnp.float32)  135 us
    dot_general x119, matrix products, mixing(): lax.dot_general(piece, weight, (((1,), (1,)), ((), ())), preferred_elemen...  105 us
    dot_general x16, matrix products, step(): lax.dot_general(table, back * summed, (((1,), (1,)), ((), ())), precision...  75.5 us
    concatenate x16, local copies, waits for them, and re-layouts, mixing(): return jnp.concatenate(outs, axis=1)  64.2 us
    add x16, other arithmetic, step(): return (carry + message, dradial)  64.1 us
    gather x16, local copies, waits for them, and re-layouts, step(): index = order[choose % filled]  55.9 us
    dot_general x16, matrix products, step(): lax.dot_general(rad4, table, (((0,), (0,)), ((), ())), precision=hp)  51.2 us
    gather x16, local copies, waits for them, and re-layouts, step(): other = pool_feat[index]  44.7 us
  transfers between devices with their start and end apart: 4, of which 3 were waited for; matrix products, arithmetic and copies ran while one was open for 6% of the time, Pallas kernels for 0%

commit v1 on v0

v1 whole, which is shorter than its diff:
```python
import functools
import math

import jax
import jax.numpy as jnp
import numpy as np
from jax import lax
from jax.experimental import pallas as pl
from jax.experimental.pallas import tpu as pltpu
from jax.sharding import PartitionSpec as P

DEGREES = (0, 1, 2, 3, 1, 2, 3, 1, 2, 3, 2, 3, 2, 3, 3, 3)
AXES = ("gx", "gy", "gz")
GROUPS = ((0, 4), (4, 10), (10, 14), (14, 16))
TILE = 32
VMEM_LIMIT = 48 * 1024 * 1024


def degree_columns(chans):
    return np.repeat(np.asarray(DEGREES), chans)


def dotf(a, b, ca=1, cb=0):
    return lax.dot_general(a, b, (((ca,), (cb,)), ((), ())), preferred_element_type=jnp.float32)


def twice(matrix):
    zero = jnp.zeros_like(matrix)
    return jnp.concatenate(
        [jnp.concatenate([matrix, zero], 1), jnp.concatenate([zero, matrix], 1)], 0
    )


def edges(start, feat_ref, nbr_ref, rad_ref, spread_ref, nbr_count):
    pool = feat_ref.shape[0]
    lane = lax.broadcasted_iota(jnp.int32, (TILE, pool), 1)
    row = lax.broadcasted_iota(jnp.int32, (TILE, pool), 0) + start
    own = jnp.where(lane == row, 1.0, 0.0)
    nbr = nbr_ref[pl.ds(start, TILE), :].astype(jnp.int32)
    rad = rad_ref[pl.ds(start, TILE), :].astype(jnp.float32)
    half = 4 * nbr_count
    which = lax.broadcasted_iota(jnp.int32, (TILE, 2 * half), 1) % half // 4
    picks, rads = [], []
    for k in range(nbr_count):
        picks.append((own + jnp.where(lane == nbr[:, k : k + 1], 1.0, 0.0)).astype(jnp.bfloat16))
        rads.append(jnp.where(which == k, rad, 0.0).astype(jnp.bfloat16))
    y = dotf(jnp.concatenate(picks, 0), feat_ref[...])
    scale = dotf(jnp.concatenate(rads, 0), spread_ref[...])
    return y, (y * scale).astype(jnp.bfloat16)


def forward_kernel(
    nbr_count,
    chans,
    got_ref,
    nbrs_ref,
    radial_ref,
    spread_ref,
    f0, f1, f2, f3, s0, s1, s2, s3,
    base_ref,
    feat_ref,
    perm_ref,
    nbr_ref,
    rad_ref,
    count_ref,
):
    pool = got_ref.shape[0]
    width = 16 * chans
    ri = lax.broadcasted_iota(jnp.int32, (pool, pool), 0)
    ci = lax.broadcasted_iota(jnp.int32, (pool, pool), 1)
    mask = got_ref[:, width:]
    upto = dotf(mask, jnp.where(ri <= ci, 1.0, 0.0).astype(jnp.bfloat16), 0, 0)
    here = dotf(mask, jnp.where(ri == ci, 1.0, 0.0).astype(jnp.bfloat16), 0, 0)
    place = jnp.where(here[0:1] > 0.5, upto[0:1], 0.0) - 1.0
    perm = jnp.where(place.astype(jnp.int32) == ri, 1.0, 0.0).astype(jnp.bfloat16)
    perm_ref[...] = perm
    total = jnp.max(upto)
    count = total.astype(jnp.int32)
    count_ref[0, 0] = count
    feat_ref[...] = dotf(perm, got_ref[:, :width]).astype(jnp.bfloat16)
    raw = nbrs_ref[...].astype(jnp.float32)
    rest = raw - jnp.floor((raw + 0.5) / total) * total
    high = jnp.floor(rest * (1.0 / 32.0))
    low = rest - 32.0 * high
    nbr_ref[...] = 32.0 * dotf(perm, high.astype(jnp.bfloat16), 1, 1) + dotf(
        perm, low.astype(jnp.bfloat16), 1, 1
    )
    radial = radial_ref[...]
    coarse = radial.astype(jnp.bfloat16)
    fine = (radial - coarse.astype(jnp.float32)).astype(jnp.bfloat16)
    both = jnp.concatenate([coarse, fine], 0)
    rad_ref[...] = dotf(perm, both, 1, 1).astype(jnp.bfloat16)
    base_ref[...] = jnp.zeros_like(base_ref)

    def body(tile, carry):
        start = pl.multiple_of(tile * TILE, TILE)
        _, z = edges(start, feat_ref, nbr_ref, rad_ref, spread_ref, nbr_count)
        for (a, b), first, second in zip(GROUPS, (f0, f1, f2, f3), (s0, s1, s2, s3)):
            a, b = a * chans, b * chans
            u = dotf(z[:, a:b], first[...])
            v = u * (0.5 + 0.5 * jnp.tanh(0.5 * u))
            v = jnp.sum(v.reshape(nbr_count, TILE, b - a), axis=0)
            near = dotf(v.astype(jnp.bfloat16), second[...])
            own = feat_ref[pl.ds(start, TILE), a:b].astype(jnp.float32)
            base_ref[pl.ds(start, TILE), a:b] = own + 0.25 * near
        return carry

    lax.fori_loop(0, (count + TILE - 1) // TILE, body, 0)


def backward_kernel(
    nbr_count,
    chans,
    count_ref,
    got_ref,
    feat_ref,
    perm_ref,
    nbr_ref,
    rad_ref,
    spread_ref,
    gather_ref,
    f0, f1, f2, f3, s0, s1, s2, s3,
    out_ref,
    trans_ref,
    grad_ref,
):
    cot = dotf(perm_ref[...], got_ref[...]).astype(jnp.bfloat16)
    for (a, b), second in zip(GROUPS, (s0, s1, s2, s3)):
        a, b = a * chans, b * chans
        trans_ref[:, a:b] = dotf(cot[:, a:b], second[...], 1, 1)
    grad_ref[...] = jnp.zeros_like(grad_ref)
    count = count_ref[0, 0]
    cols = 4 * nbr_count

    def body(tile, carry):
        start = pl.multiple_of(tile * TILE, TILE)
        y, z = edges(start, feat_ref, nbr_ref, rad_ref, spread_ref, nbr_count)
        total = jnp.zeros((nbr_count * TILE, cols), jnp.float32)
        for (a, b), first in zip(GROUPS, (f0, f1, f2, f3)):
            a, b = a * chans, b * chans
            u = dotf(z[:, a:b], first[...])
            sig = 0.5 + 0.5 * jnp.tanh(0.5 * u)
            slope = sig * (1.0 + u * (1.0 - sig))
            t = trans_ref[pl.ds(start, TILE), a:b]
            gu = slope.reshape(nbr_count, TILE, b - a) * t[None]
            gu = gu.reshape(nbr_count * TILE, b - a).astype(jnp.bfloat16)
            prod = dotf(gu, first[...], 1, 1) * y[:, a:b]
            coarse = prod.astype(jnp.bfloat16)
            fine = (prod - coarse.astype(jnp.float32)).astype(jnp.bfloat16)
            total += dotf(coarse, gather_ref[a:b, :]) + dotf(fine, gather_ref[a:b, :])
        total = total.reshape(nbr_count, TILE, cols)
        k = lax.broadcasted_iota(jnp.int32, total.shape, 0)
        col = lax.broadcasted_iota(jnp.int32, total.shape, 2)
        total = jnp.sum(jnp.where(col // 4 == k, total, 0.0), axis=0)
        grad_ref[pl.ds(start, TILE), :] = 0.25 * total
        return carry

    lax.fori_loop(0, (count + TILE - 1) // TILE, body, 0)
    rest = grad_ref[...]
    perm = perm_ref[...]
    out = jnp.zeros(out_ref.shape, jnp.float32)
    for _ in range(3):
        piece = rest.astype(jnp.bfloat16)
        rest = rest - piece.astype(jnp.float32)
        out += dotf(piece, perm, 0, 0)
    out_ref[...] = out


def vmem(count):
    return [pl.BlockSpec(memory_space=pltpu.VMEM)] * count


def shards(
    features,
    cotangent,
    leaf_device,
    neighbours,
    radial,
    first_zero,
    first_one,
    first_two,
    first_three,
    second_zero,
    second_one,
    second_two,
    second_three,
    lift_leaf,
    lift_branch,
    couple_root,
    couple_branch,
    couple_leaf,
):
    hp = lax.Precision.HIGHEST
    bf16, f32 = jnp.bfloat16, jnp.float32
    rows, width = features.shape
    chans = width // 16
    size_x, size_y, size_z = (lax.axis_size(a) for a in AXES)
    devices = size_x * size_y * size_z
    nbr_count, pool = neighbours.shape
    cap = pool // devices

    target = leaf_device[:, 0]
    onehot = (target[:, None] == jnp.arange(devices, dtype=jnp.int32)[None, :]).astype(bf16)
    before = jnp.asarray(np.tril(np.ones((rows, rows), np.float32), -1), bf16)
    rank = jnp.sum(dotf(before, onehot) * onehot.astype(f32), axis=1).astype(jnp.int32)
    slot = target * cap + rank
    place = (slot[:, None] == jnp.arange(pool, dtype=jnp.int32)[None, :]).astype(bf16)

    def exchange(block):
        block = block.astype(bf16).reshape(devices, cap, block.shape[1])
        out = lax.all_to_all(block, AXES, split_axis=0, concat_axis=0, tiled=True)
        return out.reshape(pool, block.shape[2])

    marked = jnp.concatenate([features, jnp.ones((rows, 128), bf16)], axis=1)
    got_feat = exchange(dotf(place, marked, 0, 0))
    got_cot = exchange(dotf(place, cotangent, 0, 0))

    firsts = (first_zero, twice(first_one), twice(first_two), twice(first_three))
    seconds = (second_zero, twice(second_one), twice(second_two), twice(second_three))
    degrees = degree_columns(chans)
    cols = 4 * nbr_count
    match = (np.arange(cols)[:, None] % 4 == degrees[None, :]).astype(np.float32)
    spread = jnp.asarray(np.concatenate([match, match], 0), bf16)
    collect = jnp.asarray(match.T, bf16)

    shape = jax.ShapeDtypeStruct
    params = pltpu.CompilerParams(vmem_limit_bytes=VMEM_LIMIT)
    edge_flops = 2 * pool * nbr_count * width * 1024
    base, feat, perm, nbr, rad, count = pl.pallas_call(
        functools.partial(forward_kernel, nbr_count, chans),
        out_shape=(
            shape((pool, width), f32),
            shape((pool, width), bf16),
            shape((pool, pool), bf16),
            shape((pool, nbr_count), f32),
            shape((pool, 2 * cols), bf16),
            shape((1, 1), jnp.int32),
        ),
        in_specs=vmem(12),
        out_specs=tuple(vmem(5)) + (pl.BlockSpec(memory_space=pltpu.SMEM),),
        compiler_params=params,
        cost_estimate=pl.CostEstimate(
            flops=edge_flops, bytes_accessed=8 << 20, transcendentals=pool * nbr_count * width
        ),
        name="edge_forward",
    )(got_feat, neighbours, radial, spread, *firsts, *seconds)

    leaf = jnp.sum(got_feat[:, :width], axis=0, dtype=f32).reshape(16, chans) / math.sqrt(rows)
    tiles = lax.all_gather(leaf[None], AXES, axis=0, tiled=True)
    tiles = tiles.reshape(size_x, size_y, size_z, 16, chans)
    index_x, index_y, index_z = (lax.axis_index(a) for a in AXES)
    root_w = couple_root[index_x] * (jnp.arange(size_x) != index_x)[:, None, None]
    branch_w = couple_branch[index_y] * (jnp.arange(size_y) != index_y)[:, None, None]
    leaf_w = couple_leaf[index_z] * (jnp.arange(size_z) != index_z)[:, None, None]
    branches = jnp.einsum("zpq,xyzqc->xypc", lift_leaf, tiles, precision=hp)
    roots = jnp.einsum("ypq,xyqc->xpc", lift_branch, branches, precision=hp)
    local1 = jnp.einsum("xpq,xqc->pc", root_w, roots, precision=hp)
    local2 = jnp.einsum("qp,qc->pc", lift_branch[index_y], local1, precision=hp) + jnp.einsum(
        "ypq,yqc->pc", branch_w, branches[index_x], precision=hp
    )
    local3 = jnp.einsum("qp,qc->pc", lift_leaf[index_z], local2, precision=hp) + jnp.einsum(
        "zpq,zqc->pc", leaf_w, tiles[index_x, index_y], precision=hp
    )
    out_c = (base + feat.astype(f32) * local3.reshape(1, width)).astype(bf16)
    returned = exchange(dotf(perm, out_c, 0, 0))

    grads = pl.pallas_call(
        functools.partial(backward_kernel, nbr_count, chans),
        out_shape=shape((cols, pool), f32),
        in_specs=[pl.BlockSpec(memory_space=pltpu.SMEM)] + vmem(15),
        out_specs=vmem(1)[0],
        scratch_shapes=[pltpu.VMEM((pool, width), f32), pltpu.VMEM((pool, cols), f32)],
        compiler_params=params,
        cost_estimate=pl.CostEstimate(
            flops=2 * edge_flops, bytes_accessed=8 << 20, transcendentals=pool * nbr_count * width
        ),
        name="edge_backward",
    )(count, got_cot, feat, perm, nbr, rad, spread, collect, *firsts, *seconds)

    updated = dotf(place, returned).astype(bf16)
    return (updated, grads)


def solution(mesh):
    split = P(AXES, None)
    across = P(None, AXES)
    placed = (split, split, split, across, across) + (P(),) * 13
    return jax.shard_map(
        shards,
        mesh=mesh,
        in_specs=placed,
        out_specs=(split, across),
        check_vma=False,
    )
```

time: 848 us -> 212 us (0.25); the launches traced: 832 us -> 208 us
  matrix products: 371 us -> 15.5 us
  local copies, waits for them, and re-layouts: 214 us -> 17.9 us
  other arithmetic: 164 us -> 2.57 us
  Pallas kernels: 0 us -> 80.7 us
  blocking collectives: 18.9 us -> 47.5 us
  starting transfers between devices: 29.7 us -> 20.5 us
    dot_general x380 -> x10, matrix products: 370 us -> 15 us  [the longest x5 11.3 us: dotf(): lax.dot_general(a, b, (((ca,), (cb,)), ((), ())), preferred_element_type=...]
    gather x33 -> x0, local copies, waits for them, and re-layouts: 103 us -> none  [the longest x16 55.9 us: step(): index = order[choose % filled]]
    pallas_call x0 -> x2, Pallas kernels: none -> 80.7 us  [the longest x1 46.7 us: shards(): pl.pallas_call(functools.partial(backward_kernel, nbr_count, chans), out_...]
    concatenate x16 -> x0, local copies, waits for them, and re-layouts: 64.2 us -> none  [mixing(): return jnp.concatenate(outs, axis=1)]
    add x16 -> x1, other arithmetic: 64.1 us -> 0.69 us  [shards(): slot = target * cap + rank]
    all_to_all x6 -> x0, other arithmetic: 44.8 us -> none  [the longest x2 16.7 us: shards(): lax.all_to_all(send_grad.reshape(flat_shape), ('gx', 'gy', 'gz'), split_a...]
    convert_element_type x20 -> x4, other arithmetic: 32.9 us -> 0.02 us  [the longest x1 0.01 us: shards(): jnp.sum(dotf(before, onehot) * onehot.astype(f32), axis=1).astype(jnp.int32)]
    all_gather x3 -> x1, blocking collectives: 18.9 us -> 47.5 us  [shards(): tiles = lax.all_gather(leaf[None], AXES, axis=0, tiled=True)]
  transfers between devices with their start and end apart: 4 -> 3, of which waited for: 3 -> 1; matrix products, arithmetic and copies ran while one was open for 6% -> 5% of each run, Pallas kernels for 0% -> 39%
where the time goes in v1:
time: 212 us; the launch traced here: 208 us
  Pallas kernels  80.7 us (38%)
  blocking collectives  47.5 us (22%)
  waiting for transfers between devices  22.8 us (11%)
  starting transfers between devices  20.5 us (10%)
  local copies, waits for them, and re-layouts  17.9 us (8%)
  matrix products  15.5 us (7%)
  other arithmetic  2.57 us (1%)
    all_gather x1, blocking collectives, shards(): tiles = lax.all_gather(leaf[None], AXES, axis=0, tiled=True)  47.5 us
    pallas_call x1, Pallas kernels, shards(): pl.pallas_call(functools.partial(backward_kernel, nbr_count, chans), out_...  46.7 us
    pallas_call x1, Pallas kernels, shards(): pl.pallas_call(functools.partial(forward_kernel, nbr_count, chans), out_s...  34 us
    all_to_all x3, waiting for transfers between devices, exchange(): out = lax.all_to_all(block, AXES, split_axis=0, concat_axis=0, tiled=True)  22.8 us
    all_to_all x3, starting transfers between devices, exchange(): out = lax.all_to_all(block, AXES, split_axis=0, concat_axis=0, tiled=True)  20.5 us
    unnamed x66, local copies, waits for them, and re-layouts  17.7 us
    dot_general x5, matrix products, dotf(): lax.dot_general(a, b, (((ca,), (cb,)), ((), ())), preferred_element_type=...  11.3 us
  transfers between devices with their start and end apart: 3, of which 1 were waited for; matrix products, arithmetic and copies ran while one was open for 5% of the time, Pallas kernels for 39%

profile of v1, /device:TPU:27, one launch (start us, length us, event | category | flops | bytes accessed | tf_op | source)
XLA Modules:
  0.0 208.3 jit_solution(11495598681806993894)
XLA Ops:
  0.7 1.2 fusion
  2.6 2.8 %convolution_convert_fusion = bf16[512,1152]{1,0:T(8,128)(2,1)} fusion(bf16[256,1024]{1,0:T(8,128)(2,1)} %param.21, s32[256]{0:T(256)S(1)} %bitcast.74), kind=kOutput, calls=%fused_computation | convolution fusion | flops 302710784 | bytes 1704960 | tf_op jit(solution)/shard_map/dot_general | solution.py:24
  5.3 6.2 %all-to-all-start = ((bf16[32,16,1152]{2,1,0:T(8,128)(2,1)}), bf16[32,16,1152]{2,1,0:T(8,128)(2,1)S(1)}, u32[]{:S(2)}, u32[]{:S(2)}) async-start(bf16[32,16,1152]{2,1,0:T(8,128)(2,1)} %bitcast.3), calls=%async_computation | async-start | bytes 2359296 | tf_op jit(solution)/shard_map/all_to_all | solution.py:211
  12.3 1.0 fusion.7
  13.3 1.5 convolution_convert_fusion.1
  14.8 22.8 %all-to-all-done = bf16[32,16,1152]{2,1,0:T(8,128)(2,1)S(1)} async-done(((bf16[32,16,1152]{2,1,0:T(8,128)(2,1)}), bf16[32,16,1152]{2,1,0:T(8,128)(2,1)S(1)}, u32[]{:S(2)}, u32[]{:S(2)}) %all-to-all-start) | async-done | bytes 1179680 | tf_op jit(solution)/shard_map/all_to_all | solution.py:211
  37.6 6.6 %all-to-all-start.2 = ((bf16[32,16,1024]{2,1,0:T(8,128)(2,1)}), bf16[32,16,1024]{2,1,0:T(8,128)(2,1)S(1)}, u32[]{:S(2)}, u32[]{:S(2)}) async-start(bf16[32,16,1024]{2,1,0:T(8,128)(2,1)} %bitcast.69), calls=%async_computation.2 | async-start | bytes 2097152 | tf_op jit(solution)/shard_map/all_to_all | solution.py:211
  44.5 47.5 %all_gather.3 = f32[32,16,64]{2,1,0:T(8,128)S(1)} all-gather(f32[1,16,64]{2,1,0:T(8,128)S(1)} %div.10), channel_id=1, replica_groups=mesh['gx'=4,'gy'=4,'gz'=2] {'gx','gy','gz'}, dimensions={0}, use_global_device_ids=true | all-gather | bytes 135168 | tf_op jit(solution)/shard_map/all_gather | solution.py:249
  92.4 1.0 convolution_bitcast_fusion
  93.4 1.0 convolution_bitcast_fusion.3
  94.4 1.1 convolution_bitcast_fusion.2
  96.3 1.0 copy-done.3
  97.3 1.0 copy-done.5
  103.2 0.9 copy-done.17
  104.2 34.0 %edge_forward.1 = (f32[512,1024]{1,0:T(8,128)}, bf16[512,1024]{1,0:T(8,128)(2,1)S(1)}, bf16[512,512]{1,0:T(8,128)(2,1)S(1)}, f32[512,16]{1,0:T(8,128)S(1)}, bf16...) custom-call(bf16[512,1152]{1,0:T(8,128)(2,1)S(1)} %bitcast.67, s32[16,512]{1,0:T(8,128)S(1)} %copy-done.16, ...), custom_call_target="tpu_custom_call" | custom-call | flops 17179869184 | bytes 8388608 | tf_op jit(solution)/shard_map/edge_forward/pallas_call | solution.py:229
  139.5 3.3 %convolution_convert_fusion.2 = bf16[512,1024]{1,0:T(8,128)(2,1)} fusion(bf16[512,512]{1,0:T(8,128)(2,1)S(1)} %get-tuple-element.8.perm_ref, f32[512,1024]{1,0:T(8,128)} %get-tuple-element.9, bf16[512,1024]{1,0:T(8,128)(2,1)S(1)} %get-tuple-element.10.feat_ref, f32[1024]{0:T(1024)S(1)} %mul.53), kind=kOutput, calls=%fused_computation.4 | convolution fusion | flops 539492352 | bytes 4722688 | tf_op jit(solution)/shard_map/dot_general | solution.py:24
  142.9 1.0 copy-done.1
  143.8 7.7 %all-to-all-start.1 = ((bf16[32,16,1024]{2,1,0:T(8,128)(2,1)}), bf16[32,16,1024]{2,1,0:T(8,128)(2,1)}, u32[]{:S(2)}, u32[]{:S(2)}) async-start(bf16[32,16,1024]{2,1,0:T(8,128)(2,1)} %bitcast.70), calls=%async_computation.1 | async-start | bytes 2097152 | tf_op jit(solution)/shard_map/all_to_all | solution.py:211
  151.6 1.0 copy-done.4
  152.6 1.0 copy-done.6
  156.3 0.9 copy-done.19
  157.3 0.9 copy-done.21
  159.1 46.7 %edge_backward.1 = f32[64,512]{1,0:T(8,128)} custom-call(s32[1,1]{1,0:T(1,128)} %get-tuple-element.11.count_ref, bf16[512,1024]{1,0:T(8,128)(2,1)S(1)} %bitcast.68, bf16[512,1024]{1,0:T(8,128)(2,1)S(1)} %copy-done.2, bf16[512,512]{1,0:T(8,128)(2,1)S(1)} %get-tuple-element.8.perm_ref, f32[512,16]{1,0:T(8,128)S(1)} %copy-done.21, ...), custom_call_target="tpu_custom_call" | custom-call | flops 34359738368 | bytes 8388608 | tf_op jit(solution)/shard_map/edge_backward/pallas_call | solution.py:267
  205.8 2.5 %convolution_convert_fusion.3 = bf16[256,1024]{1,0:T(8,128)(2,1)} fusion(bf16[512,1024]{1,0:T(8,128)(2,1)} %bitcast.27, s32[256]{0:T(256)S(1)} %bitcast.76), kind=kOutput, calls=%fused_computation.5 | convolution fusion | flops 268828672 | bytes 1573888 | tf_op jit(solution)/shard_map/dot_general | solution.py:24
  (75 shorter events, 12.8 us)
Async XLA Ops:
  0.6 12.7 %copy-start = (bf16[256,1024]{1,0:T(8,128)(2,1)S(1)}, bf16[256,1024]{1,0:T(8,128)(2,1)}, u32[]{:S(2)}) copy-start(bf16[256,1024]{1,0:T(8,128)(2,1)} %param.22) | copy-start | bytes 1572868
  0.6 10.9 %copy-start.30 = (bf16[64,64]{1,0:T(8,128)(2,1)S(1)}, bf16[64,64]{1,0:T(8,128)(2,1)}, u32[]{:S(2)}) copy-start(bf16[64,64]{1,0:T(8,128)(2,1)} %param.29) | copy-start | bytes 24580
  0.7 10.9 %copy-start.31 = (bf16[64,64]{1,0:T(8,128)(2,1)S(1)}, bf16[64,64]{1,0:T(8,128)(2,1)}, u32[]{:S(2)}) copy-start(bf16[64,64]{1,0:T(8,128)(2,1)} %param.33) | copy-start | bytes 24580
  2.5 9.7 %copy-start.28 = (bf16[128,128]{1,0:T(8,128)(2,1)S(1)}, bf16[128,128]{1,0:T(8,128)(2,1)}, u32[]{:S(2)}) copy-start(bf16[128,128]{1,0:T(8,128)(2,1)} %param.28) | copy-start | bytes 98308
  2.5 9.7 %copy-start.29 = (bf16[128,128]{1,0:T(8,128)(2,1)S(1)}, bf16[128,128]{1,0:T(8,128)(2,1)}, u32[]{:S(2)}) copy-start(bf16[128,128]{1,0:T(8,128)(2,1)} %param.32) | copy-start | bytes 98308
  2.5 9.8 %copy-start.24 = (bf16[192,192]{1,0:T(8,128)(2,1)S(1)}, bf16[192,192]{1,0:T(8,128)(2,1)}, u32[]{:S(2)}) copy-start(bf16[192,192]{1,0:T(8,128)(2,1)} %param.27) | copy-start | bytes 221188
  2.5 9.8 %copy-start.25 = (bf16[192,192]{1,0:T(8,128)(2,1)S(1)}, bf16[192,192]{1,0:T(8,128)(2,1)}, u32[]{:S(2)}) copy-start(bf16[192,192]{1,0:T(8,128)(2,1)} %param.31) | copy-start | bytes 221188
  5.3 32.3 %all-to-all-start = ((bf16[32,16,1152]{2,1,0:T(8,128)(2,1)}), bf16[32,16,1152]{2,1,0:T(8,128)(2,1)S(1)}, u32[]{:S(2)}, u32[]{:S(2)}) async-start(bf16[32,16,1152]{2,1,0:T(8,128)(2,1)} %bitcast.3), calls=%async_computation | async-start | bytes 2359296 | tf_op jit(solution)/shard_map/all_to_all | solution.py:211
  14.8 77.2 %copy-start.27 = (f32[2,16,16]{2,1,0:T(8,128)S(1)}, f32[2,16,16]{2,1,0:T(8,128)}, u32[]{:S(2)}) copy-start(f32[2,16,16]{2,1,0:T(8,128)} %param.34) | copy-start | bytes 6148
  14.8 77.5 %copy-start.26 = (f32[4,16,16]{2,1,0:T(8,128)S(1)}, f32[4,16,16]{2,1,0:T(8,128)}, u32[]{:S(2)}) copy-start(f32[4,16,16]{2,1,0:T(8,128)} %param.35) | copy-start | bytes 12292
  37.6 58.1 %copy-start.32 = (f32[2,2,16,16]{3,2,1,0:T(8,128)S(1)}, f32[2,2,16,16]{3,2,1,0:T(8,128)}, u32[]{:S(2)}) copy-start(f32[2,2,16,16]{3,2,1,0:T(8,128)} %param.38) | copy-start | bytes 12292
  37.6 106.2 %all-to-all-start.2 = ((bf16[32,16,1024]{2,1,0:T(8,128)(2,1)}), bf16[32,16,1024]{2,1,0:T(8,128)(2,1)S(1)}, u32[]{:S(2)}, u32[]{:S(2)}) async-start(bf16[32,16,1024]{2,1,0:T(8,128)(2,1)} %bitcast.69), calls=%async_computation.2 | async-start | bytes 2097152 | tf_op jit(solution)/shard_map/all_to_all | solution.py:211
  96.3 1.0 copy-start.3
  97.3 1.0 copy-start.5
  103.2 0.9 copy-start.17
  142.9 1.0 copy-start.1
  143.8 7.8 %copy-start.8 = (bf16[128,128]{1,0:T(8,128)(2,1)S(1)}, bf16[128,128]{1,0:T(8,128)(2,1)}, u32[]{:S(2)}) copy-start(bf16[128,128]{1,0:T(8,128)(2,1)} %get-tuple-element.18.f3) | copy-start | bytes 98308
  143.8 7.8 %copy-start.10 = (bf16[128,128]{1,0:T(8,128)(2,1)S(1)}, bf16[128,128]{1,0:T(8,128)(2,1)}, u32[]{:S(2)}) copy-start(bf16[128,128]{1,0:T(8,128)(2,1)} %get-tuple-element.19.s3) | copy-start | bytes 98308
  143.8 7.8 %copy-start.2 = (bf16[512,1024]{1,0:T(8,128)(2,1)S(1)}, bf16[512,1024]{1,0:T(8,128)(2,1)}, u32[]{:S(2)}) copy-start(bf16[512,1024]{1,0:T(8,128)(2,1)} %copy-done.1) | copy-start | bytes 3145732
  143.8 61.9 %all-to-all-start.1 = ((bf16[32,16,1024]{2,1,0:T(8,128)(2,1)}), bf16[32,16,1024]{2,1,0:T(8,128)(2,1)}, u32[]{:S(2)}, u32[]{:S(2)}) async-start(bf16[32,16,1024]{2,1,0:T(8,128)(2,1)} %bitcast.70), calls=%async_computation.1 | async-start | bytes 2097152 | tf_op jit(solution)/shard_map/all_to_all | solution.py:211
  151.6 1.0 copy-start.4
  152.6 1.0 copy-start.6
  155.4 0.9 copy-start.18
  156.3 0.9 copy-start.19
  (12 other events, 10.0 us)
